TPU v7x, 32 devices: a whole 2x2x4 slice. The times are simulated.
32 devices in a mesh: parts: 2 (over x), tile: 16 (over z, y, core).
Axes of the slice: x: 2, y: 2, z: 4, core: 2. Of those that a mesh axis runs over, the one named last changes fastest.
Arguments:
- planes: bfloat16 [3, 256, 2048], P(None, ('parts', 'tile')), parts along dimension 1, may hold values from -9 to 9
- decoder_in: float32 [32, 64], replicated, may hold values from -1 to 1
- decoder_out: float32 [64, 4], replicated, may hold values from -3 to 3
- corner: int32 [3, 2097152], P(None, ('parts', 'tile')), parts along dimension 1, may hold values from 0 to 48
- fraction: float32 [3, 2, 2097152], P(None, None, ('parts', 'tile')), parts along dimension 2, may hold values from 0 to 1
- block_slot: int32 [3, 16384], P(None, ('parts', 'tile')), parts along dimension 1, may hold values from 0 to 15, as said below
- wanted: int32 [32, 3, 16, 1], P(('parts', 'tile')), parts along dimension 0, may hold values from 0 to 7, as said below
- ray_id: int32 [32, 65536], P(('parts', 'tile')), parts along dimension 0, may hold values from 0 to 255, never falling along the last dimension, each value on 1 to 512 neighbouring positions
- ray_grad: float32 [32, 4, 256], P(('parts', 'tile')), parts along dimension 0, may hold values from -6 to 6
Outputs:
- plane_grad: float32 [3, 256, 2048], P(None, ('parts', 'tile')), parts along dimension 1
There are 2 independent parts, one for each index of `parts`. A program takes and returns all parts, laid end to end along the dimension named above; an argument that names none is the same for every part. Nothing has to cross between parts.
Inputs may be any that keep to these rules, and one draw needn't show every extreme that they name: `wanted`: for each requesting device, plane and owner, the 1 entries are distinct. `block_slot`: the 512 blocks of one device name every one of its 16 list entries at least once, for each plane.
All inputs are finite; a program needn't handle non-finite values.
Results may differ from a plain program's by a relative error of at most 0.0062.
Values may be sent and summed in bfloat16 or wider, within the bound.
A program may use at most 64 MiB of HBM per device.

v0:
```python
import jax
import jax.numpy as jnp
from jax import lax
from jax.sharding import PartitionSpec as P

OUTS = 4
TS = 8
BLK = 128


group_blocks = 16


def bilinear_matrix(group_corner, group_fraction, cell_count):
    corner_cell = group_corner // (TS - 1) * TS + group_corner % (TS - 1)
    across = group_fraction[0]
    downward = group_fraction[1]
    weights = [
        (1.0 - across) * (1.0 - downward),
        across * (1.0 - downward),
        (1.0 - across) * downward,
        across * downward,
    ]
    offsets = [0, 1, TS, TS + 1]
    places = jnp.arange(cell_count, dtype=jnp.int32)
    matrix = jnp.zeros(group_corner.shape + (cell_count,), jnp.bfloat16)
    nothing = jnp.zeros((), jnp.bfloat16)
    for weight, offset in zip(weights, offsets):
        hit = places == (corner_cell + offset)[..., None]
        matrix = matrix + jnp.where(hit, weight.astype(jnp.bfloat16)[..., None], nothing)
    return matrix


def shards(planes, decoder_in, decoder_out, corner, fraction, block_slot, wanted, ray_id, ray_grad):
    owners = lax.axis_size("tile")
    tiles_dev = planes.shape[1]
    row_len = planes.shape[2]
    per_owner = wanted.shape[3]
    channels = decoder_in.shape[0]
    cell_count = row_len // channels
    blocks = block_slot.shape[1]
    slot_count = owners * per_owner
    groups = blocks // group_blocks
    rays_dev = ray_grad.shape[2]
    served = lax.all_to_all(wanted, "tile", split_axis=2, concat_axis=0, tiled=True)
    served = jnp.transpose(served[:, :, 0, :], (1, 0, 2))
    local_ids = jnp.arange(tiles_dev, dtype=jnp.int32)
    serve_pick = (served[..., None] == local_ids).astype(jnp.bfloat16)
    outgoing = jnp.einsum(
        "pock,pkf->pocf", serve_pick, planes, preferred_element_type=jnp.float32
    ).astype(jnp.bfloat16)
    incoming = lax.all_to_all(outgoing, "tile", split_axis=1, concat_axis=1, tiled=True)
    slot_data = incoming.reshape(3, slot_count, row_len)
    slots_in = jnp.transpose(block_slot.reshape(3, groups, group_blocks), (1, 0, 2))
    corners_in = jnp.transpose(corner.reshape(3, groups, group_blocks, BLK), (1, 0, 2, 3))
    fractions_in = jnp.transpose(fraction.reshape(3, 2, groups, group_blocks, BLK), (2, 0, 1, 3, 4))
    rays_in = ray_id[0].reshape(groups, group_blocks * BLK)
    ray_table = ray_grad[0]
    slot_places = jnp.arange(slot_count, dtype=jnp.int32)
    ray_places = jnp.arange(rays_dev, dtype=jnp.int32)

    def group_step(slot_sums, inputs):
        group_slots, group_corner, group_fraction, group_rays = inputs
        matrices, features, slot_picks = ([], [], [])
        for which in range(3):
            slot_pick = slot_places[:, None] == group_slots[which][None, :]
            block_pick = jnp.transpose(slot_pick).astype(jnp.bfloat16)
            tile_block = jnp.dot(
                block_pick, slot_data[which], preferred_element_type=jnp.float32
            ).astype(jnp.bfloat16)
            tile_block = tile_block.reshape(group_blocks, channels, cell_count)
            matrix = bilinear_matrix(group_corner[which], group_fraction[which], cell_count)
            features.append(
                jnp.einsum("bck,bsk->bcs", tile_block, matrix, preferred_element_type=jnp.float32)
            )
            matrices.append(matrix)
            slot_picks.append(slot_pick.astype(jnp.float32))
        product = features[0] * features[1] * features[2]
        pre = jnp.einsum("ch,bcs->bhs", decoder_in, product, precision=lax.Precision.HIGHEST)
        ray_pick = (ray_places[:, None] == group_rays[None, :]).astype(jnp.float32)
        out_grad = jnp.dot(ray_table, ray_pick, precision=lax.Precision.HIGHEST).reshape(
            OUTS, group_blocks, BLK
        )
        hidden_grad = jnp.einsum(
            "ho,obs->bhs", decoder_out, out_grad, precision=lax.Precision.HIGHEST
        )
        sigmoid_pre = jax.nn.sigmoid(pre)
        pre_grad = hidden_grad * sigmoid_pre * (1.0 + pre * (1.0 - sigmoid_pre))
        prod_grad = jnp.einsum("ch,bhs->bcs", decoder_in, pre_grad, precision=lax.Precision.HIGHEST)
        updated = []
        for which in range(3):
            others = features[(which + 1) % 3] * features[(which + 2) % 3]
            feat_grad = (prod_grad * others).astype(jnp.bfloat16)
            block_grads = jnp.einsum(
                "bcs,bsk->bck", feat_grad, matrices[which], preferred_element_type=jnp.float32
            )
            added = jnp.dot(
                slot_picks[which],
                block_grads.reshape(group_blocks, row_len),
                precision=lax.Precision.HIGHEST,
            )
            updated.append(slot_sums[which] + added)
        return (jnp.stack(updated), None)

    start = jnp.zeros((3, slot_count, row_len), jnp.float32)
    slot_sums, unused = lax.scan(group_step, start, (slots_in, corners_in, fractions_in, rays_in))
    returned = lax.all_to_all(
        slot_sums.reshape(3, owners, per_owner, row_len),
        "tile",
        split_axis=1,
        concat_axis=1,
        tiled=True,
    )
    returned = returned.reshape(3, slot_count, row_len)
    local_places = jnp.arange(tiles_dev, dtype=jnp.int32)[None, :, None]
    owner_pick = (local_places == served.reshape(3, 1, slot_count)).astype(jnp.float32)
    plane_grad = jnp.einsum("pts,psf->ptf", owner_pick, returned, precision=lax.Precision.HIGHEST)
    return plane_grad


def solution(mesh):
    placed = (
        P(None, ("parts", "tile"), None),
        P(),
        P(),
        P(None, ("parts", "tile")),
        P(None, None, ("parts", "tile")),
        P(None, ("parts", "tile")),
        P(("parts", "tile"), None, None, None),
        P(("parts", "tile"), None),
        P(("parts", "tile"), None, None),
    )
    return jax.shard_map(
        shards,
        mesh=mesh,
        in_specs=placed,
        out_specs=P(None, ("parts", "tile"), None),
        check_vma=False,
    )
```

profile of v0, /device:TPU:0, one launch (start us, length us, event | category | flops | bytes accessed | tf_op | source)
XLA Modules:
  0.0 294.0 jit_solution(11892756249032019788)
XLA Ops:
  0.0 0.8 copy.34
  0.8 13.6 %all_to_all.25 = s32[1,3,16,1]{1,3,0,2:T(1,128)S(1)} all-to-all(s32[1,3,16,1]{1,3,0,2:T(1,128)S(1)} %copy.34), channel_id=1, replica_groups=mesh['parts'=2,'tile'=16] {'tile'}, dimensions={2} | all-to-all | bytes 384 | tf_op jit(solution)/shard_map/all_to_all | solution.py:45
  14.7 0.9 copy.36
  15.6 3.5 %all-to-all-start.1 = ((bf16[3,16,1,2048]{3,0,2,1:T(4,128)(2,1)}), bf16[3,16,1,2048]{3,0,2,1:T(4,128)(2,1)S(1)}, u32[]{:S(2)}, u32[]{:S(2)}) async-start(bf16[3,16,1,2048]{3,0,2,1:T(4,128)(2,1)} %copy.36), calls=%async_computation.1 | async-start | bytes 524288 | tf_op jit(solution)/shard_map/all_to_all | solution.py:52
  19.1 0.9 reshape.617
  20.6 2.2 reduce.3
  22.9 1.3 copy.50
  24.2 2.5 reshape.620
  26.7 2.4 all-to-all-done.1
  29.4 247.6 %while.15 = (s32[]{:T(128)}, f32[3,16,2048]{2,1,0:T(8,128)S(1)}, s32[32,3,16]{2,0,1:T(8,128)S(1)}, s32[32,2048]{1,0:T(8,128)S(1)}, f32[4,256]{1,0:T(4,128)S(1)},...) while((s32[]{:T(128)}, f32[3,16,2048]{2,1,0:T(8,128)S(1)}, ...), condition=%wide.region_1.2_spmd.clone.clone, body=%wide.region_0.1_spmd.clone.clone.sunk | while | flops 219913728 | bytes 11255037 | solution.py:106
  29.4 0.8 fusion.162
  30.2 0.8 dynamic-slice_bitcast_fusion.5
  38.0 0.8 dynamic-slice_bitcast_fusion.5
  44.9 0.8 fusion.162
  45.7 0.8 dynamic-slice_bitcast_fusion.5
  52.6 0.8 fusion.162
  53.5 0.8 dynamic-slice_bitcast_fusion.5
  60.4 0.8 fusion.162
  61.2 0.8 dynamic-slice_bitcast_fusion.5
  68.1 0.8 fusion.162
  68.9 0.8 dynamic-slice_bitcast_fusion.5
  75.9 0.8 fusion.162
  76.7 0.8 dynamic-slice_bitcast_fusion.5
  83.6 0.8 fusion.162
  84.4 0.8 dynamic-slice_bitcast_fusion.5
  91.3 0.8 fusion.162
  92.2 0.8 dynamic-slice_bitcast_fusion.5
  99.1 0.8 fusion.162
  99.9 0.8 dynamic-slice_bitcast_fusion.5
  106.8 0.8 fusion.162
  107.6 0.8 dynamic-slice_bitcast_fusion.5
  114.5 0.8 fusion.162
  115.4 0.8 dynamic-slice_bitcast_fusion.5
  122.3 0.8 fusion.162
  123.1 0.8 dynamic-slice_bitcast_fusion.5
  130.0 0.8 fusion.162
  130.9 0.8 dynamic-slice_bitcast_fusion.5
  137.8 0.8 fusion.162
  138.6 0.8 dynamic-slice_bitcast_fusion.5
  145.5 0.8 fusion.162
  146.3 0.8 dynamic-slice_bitcast_fusion.5
  153.2 0.8 fusion.162
  154.1 0.8 dynamic-slice_bitcast_fusion.5
  161.0 0.8 fusion.162
  161.8 0.8 dynamic-slice_bitcast_fusion.5
  168.7 0.8 fusion.162
  169.5 0.8 dynamic-slice_bitcast_fusion.5
  176.5 0.8 fusion.162
  177.3 0.8 dynamic-slice_bitcast_fusion.5
  185.0 0.8 dynamic-slice_bitcast_fusion.5
  191.9 0.8 fusion.162
  192.8 0.8 dynamic-slice_bitcast_fusion.5
  200.5 0.8 dynamic-slice_bitcast_fusion.5
  208.2 0.8 dynamic-slice_bitcast_fusion.5
  216.0 0.8 dynamic-slice_bitcast_fusion.5
  223.7 0.8 dynamic-slice_bitcast_fusion.5
  231.5 0.8 dynamic-slice_bitcast_fusion.5
  239.2 0.8 dynamic-slice_bitcast_fusion.5
  246.9 0.8 dynamic-slice_bitcast_fusion.5
  254.7 0.8 dynamic-slice_bitcast_fusion.5
  262.4 0.8 dynamic-slice_bitcast_fusion.5
  270.2 0.8 dynamic-slice_bitcast_fusion.5
  277.4 15.6 %all_to_all.26 = f32[3,16,1,2048]{3,2,0,1:T(1,128)S(1)} all-to-all(f32[3,16,1,2048]{3,2,0,1:T(1,128)S(1)} %copy.41), channel_id=1, replica_groups=mesh['parts'=2,'tile'=16] {'tile'}, dimensions={1} | all-to-all | bytes 786432 | tf_op jit(solution)/shard_map/all_to_all | solution.py:107
  293.0 1.0 fusion.88
  (990 shorter events, 203.5 us)
Async XLA Ops:
  0.0 14.5 %copy-start = (bf16[3,8,2048]{2,1,0:T(8,128)(2,1)S(1)}, bf16[3,8,2048]{2,1,0:T(8,128)(2,1)}, u32[]{:S(2)}) copy-start(bf16[3,8,2048]{2,1,0:T(8,128)(2,1)} %param.11) | copy-start | bytes 294916
  15.6 13.5 %all-to-all-start.1 = ((bf16[3,16,1,2048]{3,0,2,1:T(4,128)(2,1)}), bf16[3,16,1,2048]{3,0,2,1:T(4,128)(2,1)S(1)}, u32[]{:S(2)}, u32[]{:S(2)}) async-start(bf16[3,16,1,2048]{3,0,2,1:T(4,128)(2,1)} %copy.36), calls=%async_computation.1 | async-start | bytes 524288 | tf_op jit(solution)/shard_map/all_to_all | solution.py:52
  19.1 5.0 %copy-start.2 = (f32[3,2,65536]{2,1,0:T(2,128)S(1)}, f32[3,2,65536]{2,1,0:T(2,128)}, u32[]{:S(2)}) copy-start(f32[3,2,65536]{2,1,0:T(2,128)} %param.15) | copy-start | bytes 4718596
  24.2 5.2 %copy-start.1 = (f32[32,64]{1,0:T(8,128)S(1)}, f32[32,64]{1,0:T(8,128)}, u32[]{:S(2)}) copy-start(f32[32,64]{1,0:T(8,128)} %param.12) | copy-start | bytes 24580
  24.2 5.2 %copy-start.3 = (f32[1,4,256]{2,1,0:T(4,128)S(1)}, f32[1,4,256]{2,1,0:T(4,128)}, u32[]{:S(2)}) copy-start(f32[1,4,256]{2,1,0:T(4,128)} %param.19) | copy-start | bytes 12292
  24.2 5.2 %copy-start.4 = (f32[64,4]{0,1:T(4,128)S(1)}, f32[64,4]{0,1:T(4,128)}, u32[]{:S(2)}) copy-start(f32[64,4]{0,1:T(4,128)} %param.13) | copy-start | bytes 3076
where the time goes:
time: 296 us; the launch traced here: 294 us
  matrix products  186 us (63%)
  local copies, waits for them, and re-layouts  63.2 us (21%)
  blocking collectives  29.1 us (10%)
  other arithmetic  5.39 us (2%)
  loops' own time  4.66 us (2%)
  starting transfers between devices  3.53 us (1%)
    dot_general x96, matrix products, group_step(): jnp.einsum('bcs,bsk->bck', feat_grad, matrices[which], preferred_element_...  33.7 us
    dot_general x96, matrix products, group_step(): jnp.einsum('bck,bsk->bcs', tile_block, matrix, preferred_element_type=jnp...  31.6 us
    dynamic_slice x96, local copies, waits for them, and re-layouts, shards(): lax.scan(group_step, start, (slots_in, corners_in, fractions_in, rays_in))  26.6 us
    dot_general x32, matrix products, group_step(): jnp.dot(ray_table, ray_pick, precision=lax.Precision.HIGHEST)  24.1 us
    dot_general x32, matrix products, group_step(): jnp.einsum('ho,obs->bhs', decoder_out, out_grad, precision=lax.Precision....  22.8 us
    dot_general x32, matrix products, group_step(): jnp.einsum('ch,bcs->bhs', decoder_in, product, precision=lax.Precision.HI...  19.9 us
    dot_general x96, matrix products, group_step(): jnp.dot(block_pick, slot_data[which], preferred_element_type=jnp.float32)  19.7 us
    dot_general x96, matrix products, group_step(): jnp.dot(slot_picks[which], block_grads.reshape(group_blocks, row_len), pr...  19.2 us
  transfers between devices with their start and end apart: 1, of which 1 were waited for; matrix products, arithmetic and copies ran while one was open for 3% of the time, Pallas kernels for 0%

commit v1 on v0

v1 whole, which is shorter than its diff:
```python
import functools

import jax
import jax.numpy as jnp
from jax import lax
from jax.experimental import pallas as pl
from jax.experimental.pallas import tpu as pltpu
from jax.sharding import PartitionSpec as P

OUTS = 4
TS = 8
BLK = 128
CHUNK = 8192
GROUP = 16
UNROLL = 1

F32 = jnp.float32
BF16 = jnp.bfloat16


def cell_weights(corner_row, across, downward):
    row = (corner_row * 37) >> 8
    col = corner_row - row * (TS - 1)
    sub = lax.broadcasted_iota(jnp.int32, (TS, BLK), 0)
    col8 = jnp.broadcast_to(col, (TS, BLK))
    side = jnp.where(sub == col8, 1.0 - across, jnp.where(sub == col8 + 1, across, 0.0))
    upper = side * (1.0 - downward)
    lower = side * downward
    upper = jnp.concatenate([upper, upper], axis=0).astype(BF16)
    lower = jnp.concatenate([lower, lower], axis=0).astype(BF16)
    row8 = jnp.broadcast_to(row, (TS, BLK)).astype(F32)
    rows = jnp.concatenate([row8, row8 - 1.0], axis=0).astype(BF16)
    zero = jnp.zeros((2 * TS, BLK), BF16)
    pairs = []
    for first in range(0, TS, 2):
        here = rows == jnp.asarray(first, BF16)
        above = rows == jnp.asarray(first - 1, BF16)
        pairs.append(jnp.where(here, upper, jnp.where(above, lower, zero)))
    return jnp.concatenate(pairs, axis=0)


def dot(a, b):
    return jnp.dot(a, b, preferred_element_type=F32)


def dot_t(a, b):
    return lax.dot_general(a, b, (((1,), (1,)), ((), ())), preferred_element_type=F32)


def compute_kernel(
    slots_ref, tiles_ref, win_t_ref, win_ref, wout_ref, table_ref, corner_ref, fraction_ref, ray_ref, acc_ref
):
    step = pl.program_id(0)

    @pl.when(step == 0)
    def _():
        acc_ref[...] = jnp.zeros_like(acc_ref)

    halves = table_ref.shape[0]
    blocks = CHUNK // BLK

    @functools.partial(lax.fori_loop, 0, blocks // GROUP, init_val=None, unroll=UNROLL)
    def _(at, carry):
        wide, feats, slots = [], [], []
        grads_out = []
        for b in range(GROUP):
            local = at * GROUP + b
            lanes = pl.ds(pl.multiple_of(local * BLK, BLK), BLK)
            wides, fs, ss = [], [], []
            for p in range(3):
                slot = slots_ref[p, step * blocks + local]
                m = cell_weights(
                    corner_ref[p : p + 1, lanes], fraction_ref[p, 0:1, lanes], fraction_ref[p, 1:2, lanes]
                )
                z = jnp.zeros_like(m)
                w = jnp.concatenate(
                    [jnp.concatenate([m, z], axis=1), jnp.concatenate([z, m], axis=1)], axis=0
                )
                f = dot(tiles_ref[p, slot], w)
                fs.append(jnp.concatenate([f[:, :BLK], f[:, BLK:]], axis=0))
                wides.append(w)
                ss.append(slot)
            wide.append(wides)
            feats.append(fs)
            slots.append(ss)
            ray = ray_ref[0:1, lanes]
            rows = table_ref.shape[1]
            picks = []
            idx = jnp.broadcast_to(ray & (BLK - 1), (rows, BLK))
            half = jnp.broadcast_to(ray >> 7, (rows, BLK))
            sub = lax.broadcasted_iota(jnp.int32, (rows, BLK), 0) // OUTS
            for h in range(halves):
                got = jnp.take_along_axis(table_ref[h], idx, axis=1)
                picks.append(jnp.where(half == sub + 2 * h, got, 0.0))
            grads_out.append(jnp.concatenate(picks, axis=0))
        f = [jnp.concatenate([feats[b][p] for b in range(GROUP)], axis=1) for p in range(3)]
        others = [f[1] * f[2], f[0] * f[2], f[0] * f[1]]
        product = (others[2] * f[2]).astype(BF16)
        grads_out = jnp.concatenate(grads_out, axis=1).astype(BF16)
        half_pre = dot(win_t_ref[...], product)
        hidden = dot(wout_ref[...], grads_out)
        t = jnp.tanh(half_pre)
        pre_grad = hidden * ((1.0 + t) * (1.0 + half_pre * (1.0 - t)))
        prod_grad = dot(win_ref[...], pre_grad.astype(BF16))
        for p in range(3):
            fg = (prod_grad * others[p]).astype(BF16)
            half_c = fg.shape[0] // 2
            for b in range(GROUP):
                part = fg[:, b * BLK : (b + 1) * BLK]
                lhs = jnp.concatenate([part[:half_c], part[half_c:]], axis=1)
                slot = slots[b][p]
                acc_ref[p, slot] += dot_t(lhs, wide[b][p])
        return carry


def compute(slots, tiles, decoder_in, decoder_out, ray_table, corner, fraction, ray_id):
    channels, hid = decoder_in.shape
    slot_count = tiles.shape[1]
    samples = corner.shape[1]
    rays = ray_table.shape[1]
    by_parity = jnp.concatenate([decoder_in[0::2], decoder_in[1::2]], axis=0)
    win_t = (by_parity.T * 0.5).astype(BF16)
    win = by_parity.astype(BF16)
    halves = rays // (2 * BLK)
    wout = jnp.concatenate([decoder_out * 0.5] * (2 * halves), axis=1).astype(BF16)
    table = ray_table.reshape(OUTS, halves, 2, BLK).transpose(1, 2, 0, 3).reshape(halves, 2 * OUTS, BLK)
    steps = samples // CHUNK
    vmem = pl.BlockSpec(memory_space=pltpu.VMEM)
    grid_spec = pltpu.PrefetchScalarGridSpec(
        num_scalar_prefetch=1,
        grid=(steps,),
        in_specs=[
            vmem,
            vmem,
            vmem,
            vmem,
            vmem,
            pl.BlockSpec((3, CHUNK), lambda i, s: (0, i)),
            pl.BlockSpec((3, 2, CHUNK), lambda i, s: (0, 0, i)),
            pl.BlockSpec((1, CHUNK), lambda i, s: (0, i)),
        ],
        out_specs=pl.BlockSpec(tiles.shape, lambda i, s: (0, 0, 0, 0)),
    )
    return pl.pallas_call(
        compute_kernel,
        grid_spec=grid_spec,
        out_shape=jax.ShapeDtypeStruct(tiles.shape, F32),
        compiler_params=pltpu.CompilerParams(vmem_limit_bytes=48 * 1024 * 1024),
        name="field_grad",
    )(slots, tiles, win_t, win, wout, table, corner, fraction, ray_id)


def shards(planes, decoder_in, decoder_out, corner, fraction, block_slot, wanted, ray_id, ray_grad):
    owners = lax.axis_size("tile")
    tiles_dev = planes.shape[1]
    row_len = planes.shape[2]
    per_owner = wanted.shape[3]
    slot_count = owners * per_owner
    served = lax.all_to_all(wanted, "tile", split_axis=2, concat_axis=0, tiled=True)
    served = jnp.transpose(served[:, :, 0, :], (1, 0, 2))
    local_ids = jnp.arange(tiles_dev, dtype=jnp.int32)
    serve_pick = (served[..., None] == local_ids).astype(BF16)
    outgoing = jnp.einsum(
        "pock,pkf->pocf", serve_pick, planes, preferred_element_type=F32
    ).astype(BF16)
    incoming = lax.all_to_all(outgoing, "tile", split_axis=1, concat_axis=1, tiled=True)
    tiles = incoming.reshape(3, slot_count, row_len // BLK, BLK)
    slot_sums = compute(block_slot, tiles, decoder_in, decoder_out, ray_grad[0], corner, fraction, ray_id)
    returned = lax.all_to_all(
        slot_sums.reshape(3, owners, per_owner, row_len).astype(BF16),
        "tile",
        split_axis=1,
        concat_axis=1,
        tiled=True,
    )
    returned = returned.reshape(3, slot_count, row_len)
    local_places = jnp.arange(tiles_dev, dtype=jnp.int32)[None, :, None]
    owner_pick = (local_places == served.reshape(3, 1, slot_count)).astype(BF16)
    return jnp.einsum("pts,psf->ptf", owner_pick, returned, preferred_element_type=F32)


def solution(mesh):
    placed = (
        P(None, ("parts", "tile"), None),
        P(),
        P(),
        P(None, ("parts", "tile")),
        P(None, None, ("parts", "tile")),
        P(None, ("parts", "tile")),
        P(("parts", "tile"), None, None, None),
        P(("parts", "tile"), None),
        P(("parts", "tile"), None, None),
    )
    return jax.shard_map(
        shards,
        mesh=mesh,
        in_specs=placed,
        out_specs=P(None, ("parts", "tile"), None),
        check_vma=False,
    )
```

time: 296 us -> 102 us (0.34)
  matrix products: 186 us -> 1.26 us
  local copies, waits for them, and re-layouts: 63.2 us -> 5.84 us
  Pallas kernels: 0 us -> 55.4 us
  blocking collectives: 29.1 us -> 12.8 us
  waiting for transfers between devices: 2.41 us -> 14 us
  starting transfers between devices: 3.53 us -> 10.9 us
  loops' own time: 4.66 us -> 0 us
  other arithmetic: 5.39 us -> 0.75 us
    dot_general x514 -> x2, matrix products: 186 us -> 1.26 us  [the longest x1 1 us: shards(): jnp.einsum('pts,psf->ptf', owner_pick, returned, preferred_element_type=F32)]
    pallas_call x0 -> x1, Pallas kernels: none -> 55.4 us  [compute(): pl.pallas_call(compute_kernel, grid_spec=grid_spec, out_shape=jax.ShapeDt...]
    reshape x195 -> x2, local copies, waits for them, and re-layouts: 32.3 us -> 0.24 us  [shards(): tiles = incoming.reshape(3, slot_count, row_len // BLK, BLK)]
    dynamic_slice x96 -> x0, local copies, waits for them, and re-layouts: 26.6 us -> none  [shards(): lax.scan(group_step, start, (slots_in, corners_in, fractions_in, rays_in))]
    all_to_all x2 -> x1, blocking collectives: 29.1 us -> 12.8 us  [shards(): lax.all_to_all(slot_sums.reshape(3, owners, per_owner, row_len).astype(BF...]
    all_to_all x0 -> x1, starting transfers between devices: none -> 7.39 us  [shards(): lax.all_to_all(wanted, 'tile', split_axis=2, concat_axis=0, tiled=True)]
    all_to_all x1, waiting for transfers between devices: 2.41 us -> 9.19 us  [shards(): lax.all_to_all(outgoing, 'tile', split_axis=1, concat_axis=1, tiled=True)]
    all_to_all x0 -> x1, waiting for transfers between devices: none -> 4.77 us  [shards(): lax.all_to_all(wanted, 'tile', split_axis=2, concat_axis=0, tiled=True)]
  transfers between devices with their start and end apart: 1 -> 2, of which waited for: 1 -> 2; matrix products, arithmetic and copies ran while one was open for 3% -> 2% of each run, Pallas kernels for 0% -> 0%
where the time goes in v1:
time: 102 us; the launch traced here: 101 us
  Pallas kernels  55.4 us (54%)
  waiting for transfers between devices  14 us (14%)
  blocking collectives  12.8 us (13%)
  starting transfers between devices  10.9 us (11%)
  local copies, waits for them, and re-layouts  5.84 us (6%)
  matrix products  1.26 us (1%)
    pallas_call x1, Pallas kernels, compute(): pl.pallas_call(compute_kernel, grid_spec=grid_spec, out_shape=jax.ShapeDt...  55.4 us
    all_to_all x1, blocking collectives, shards(): lax.all_to_all(slot_sums.reshape(3, owners, per_owner, row_len).astype(BF...  12.8 us
    all_to_all x1, waiting for transfers between devices, shards(): lax.all_to_all(outgoing, 'tile', split_axis=1, concat_axis=1, tiled=True)  9.19 us
    all_to_all x1, starting transfers between devices, shards(): lax.all_to_all(wanted, 'tile', split_axis=2, concat_axis=0, tiled=True)  7.39 us
    all_to_all x1, waiting for transfers between devices, shards(): lax.all_to_all(wanted, 'tile', split_axis=2, concat_axis=0, tiled=True)  4.77 us
    all_to_all x1, starting transfers between devices, shards(): lax.all_to_all(outgoing, 'tile', split_axis=1, concat_axis=1, tiled=True)  3.53 us
    unnamed x14, local copies, waits for them, and re-layouts  2.74 us
  transfers between devices with their start and end apart: 2, of which 2 were waited for; matrix products, arithmetic and copies ran while one was open for 2% of the time, Pallas kernels for 0%

profile of v1, /device:TPU:0, one launch (start us, length us, event | category | flops | bytes accessed | tf_op | source)
XLA Modules:
  0.0 101.1 jit_solution(14167689714468481037)
XLA Ops:
  0.0 0.0 copy-start
  0.0 0.0 copy-start.5
  0.0 0.0 copy-start.3
  0.0 0.0 copy-start.4
  0.0 0.0 copy-start.1
  0.0 1.5 %copy.24 = s32[1,3,16,1]{1,3,0,2:T(1,128)} copy(s32[1,3,16,1]{2,3,1,0:T(1,128)} %param.15) | data formatting | bytes 384 | tf_op args[6]
  1.5 7.4 %all-to-all-start = ((s32[1,3,16,1]{1,3,0,2:T(1,128)}), s32[1,3,16,1]{1,3,0,2:T(1,128)S(1)}, u32[]{:S(2)}, u32[]{:S(2)}) async-start(s32[1,3,16,1]{1,3,0,2:T(1,128)} %copy.24), calls=%async_computation | async-start | bytes 16384 | tf_op jit(solution)/shard_map/all_to_all | solution.py:159
  8.9 0.7 slice.7
  9.6 0.7 slice.6
  10.4 0.1 copy.29.win_t_ref
  10.5 4.8 %all-to-all-done = s32[1,3,16,1]{1,3,0,2:T(1,128)S(1)} async-done(((s32[1,3,16,1]{1,3,0,2:T(1,128)}), s32[1,3,16,1]{1,3,0,2:T(1,128)S(1)}, u32[]{:S(2)}, u32[]{:S(2)}) %all-to-all-start) | async-done | bytes 224 | tf_op jit(solution)/shard_map/all_to_all | solution.py:159
  15.2 0.1 copy.25
  15.3 0.0 copy-done
  15.3 0.3 fusion
  15.6 0.9 copy.26
  16.5 3.5 %all-to-all-start.1 = ((bf16[3,16,1,2048]{3,0,2,1:T(4,128)(2,1)}), bf16[3,16,1,2048]{3,0,2,1:T(4,128)(2,1)S(1)}, u32[]{:S(2)}, u32[]{:S(2)}) async-start(bf16[3,16,1,2048]{3,0,2,1:T(4,128)(2,1)} %copy.26), calls=%async_computation.1 | async-start | bytes 524288 | tf_op jit(solution)/shard_map/all_to_all | solution.py:166
  20.0 0.7 multiply_convert_fusion.1
  20.7 0.1 copy.30.wout_ref
  20.8 9.2 %all-to-all-done.1 = bf16[3,16,1,2048]{3,0,2,1:T(4,128)(2,1)S(1)} async-done(((bf16[3,16,1,2048]{3,0,2,1:T(4,128)(2,1)}), bf16[3,16,1,2048]{3,0,2,1:T(4,128)(2,1)S(1)}, u32[]{:S(2)}, u32[]{:S(2)}) %all-to-all-start.1) | async-done | bytes 196640 | tf_op jit(solution)/shard_map/all_to_all | solution.py:166
  30.0 0.2 reshape.37
  30.3 0.0 copy-done.5
  30.3 0.0 copy-done.3
  30.3 0.0 copy-done.4
  30.3 0.0 copy-done.1
  30.3 0.0 copy-start.2
  30.3 1.2 %copy-done.2 = s32[3,65536]{1,0:T(4,128)S(1)} copy-done((s32[3,65536]{1,0:T(4,128)S(1)}, s32[3,65536]{1,0:T(4,128)}, u32[]{:S(2)}) %copy-start.2) | copy-done | bytes 786456
  31.5 55.4 %field_grad.1 = f32[3,16,16,128]{3,2,1,0:T(8,128)S(1)} custom-call(s32[3,512]{1,0:T(4,128)S(1)} %copy-done.4, bf16[3,16,16,128]{3,2,1,0:T(8,128)(2,1)S(1)} %copy.33.tiles_ref, bf16[64,32]{1,0:T(8,128)(2,1)S(1)} %copy.29.win_t_ref, bf16[32,64]{1,0:T(8,128)(2,1)S(1)} %fusion.4.win_ref, bf16[64,8]{1,0:T(8,128)(2,1)S(1)} %copy.30.wout_ref, ...), custom_call_target="tpu_custom_call" | custom-call | tf_op jit(solution)/shard_map/field_grad/pallas_call | solution.py:144
  87.0 0.1 convert_element_type.37
  87.0 0.2 copy.31
  87.2 12.8 %all_to_all.25 = bf16[3,16,1,2048]{3,0,2,1:T(4,128)(2,1)S(1)} all-to-all(bf16[3,16,1,2048]{3,0,2,1:T(4,128)(2,1)S(1)} %copy.31), channel_id=1, replica_groups=mesh['parts'=2,'tile'=16] {'tile'}, dimensions={1} | all-to-all | bytes 393216 | tf_op jit(solution)/shard_map/all_to_all | solution.py:169
  100.1 1.0 fusion.1
  (6 shorter events, 0.1 us)
Async XLA Ops:
  0.0 15.3 %copy-start = (bf16[3,8,2048]{2,1,0:T(8,128)(2,1)S(1)}, bf16[3,8,2048]{2,1,0:T(8,128)(2,1)}, u32[]{:S(2)}) copy-start(bf16[3,8,2048]{2,1,0:T(8,128)(2,1)} %param.9) | copy-start | bytes 294916
  0.0 30.3 %copy-start.5 = (f32[1,4,256]{2,1,0:T(4,128)S(1)}, f32[1,4,256]{2,1,0:T(4,128)}, u32[]{:S(2)}) copy-start(f32[1,4,256]{2,1,0:T(4,128)} %param.17) | copy-start | bytes 12292
  0.0 30.3 %copy-start.3 = (s32[1,65536]{1,0:T(1,128)S(1)}, s32[1,65536]{1,0:T(1,128)}, u32[]{:S(2)}) copy-start(s32[1,65536]{1,0:T(1,128)} %ray_ref.1) | copy-start | bytes 786436
  0.0 30.3 %copy-start.4 = (s32[3,512]{1,0:T(4,128)S(1)}, s32[3,512]{1,0:T(4,128)}, u32[]{:S(2)}) copy-start(s32[3,512]{1,0:T(4,128)} %slots_ref.1) | copy-start | bytes 18436
  0.0 30.3 %copy-start.1 = (f32[3,2,65536]{2,1,0:T(2,128)S(1)}, f32[3,2,65536]{2,1,0:T(2,128)}, u32[]{:S(2)}) copy-start(f32[3,2,65536]{2,1,0:T(2,128)} %fraction_ref.1) | copy-start | bytes 4718596
  1.5 13.7 %all-to-all-start = ((s32[1,3,16,1]{1,3,0,2:T(1,128)}), s32[1,3,16,1]{1,3,0,2:T(1,128)S(1)}, u32[]{:S(2)}, u32[]{:S(2)}) async-start(s32[1,3,16,1]{1,3,0,2:T(1,128)} %copy.24), calls=%async_computation | async-start | bytes 16384 | tf_op jit(solution)/shard_map/all_to_all | solution.py:159
  16.5 13.5 %all-to-all-start.1 = ((bf16[3,16,1,2048]{3,0,2,1:T(4,128)(2,1)}), bf16[3,16,1,2048]{3,0,2,1:T(4,128)(2,1)S(1)}, u32[]{:S(2)}, u32[]{:S(2)}) async-start(bf16[3,16,1,2048]{3,0,2,1:T(4,128)(2,1)} %copy.26), calls=%async_computation.1 | async-start | bytes 524288 | tf_op jit(solution)/shard_map/all_to_all | solution.py:166
  30.3 1.2 %copy-start.2 = (s32[3,65536]{1,0:T(4,128)S(1)}, s32[3,65536]{1,0:T(4,128)}, u32[]{:S(2)}) copy-start(s32[3,65536]{1,0:T(4,128)} %corner_ref.1) | copy-start | bytes 2359300

commit v2 on v1

--- a/solution.py
+++ b/solution.py
@@ -76,7 +76,7 @@
                 w = jnp.concatenate(
                     [jnp.concatenate([m, z], axis=1), jnp.concatenate([z, m], axis=1)], axis=0
                 )
-                f = dot(tiles_ref[p, slot], w)
+                f = dot(tiles_ref[slot, p], w)
                 fs.append(jnp.concatenate([f[:, :BLK], f[:, BLK:]], axis=0))
                 wides.append(w)
                 ss.append(slot)
@@ -109,13 +109,12 @@
                 part = fg[:, b * BLK : (b + 1) * BLK]
                 lhs = jnp.concatenate([part[:half_c], part[half_c:]], axis=1)
                 slot = slots[b][p]
-                acc_ref[p, slot] += dot_t(lhs, wide[b][p])
+                acc_ref[slot, p] += dot_t(lhs, wide[b][p])
         return carry
 
 
 def compute(slots, tiles, decoder_in, decoder_out, ray_table, corner, fraction, ray_id):
     channels, hid = decoder_in.shape
-    slot_count = tiles.shape[1]
     samples = corner.shape[1]
     rays = ray_table.shape[1]
     by_parity = jnp.concatenate([decoder_in[0::2], decoder_in[1::2]], axis=0)
@@ -150,33 +149,219 @@
     )(slots, tiles, win_t, win, wout, table, corner, fraction, ray_id)
 
 
+def peer(d, n):
+    return {"tile": lax.rem(lax.axis_index("tile") + d, n)}
+
+
+def enter(n):
+    barrier = pltpu.get_barrier_semaphore()
+
+    def tell(d, carry):
+        pl.semaphore_signal(barrier, inc=1, device_id=peer(d, n), device_id_type=pl.DeviceIdType.MESH)
+        return carry
+
+    lax.fori_loop(1, n, tell, 0)
+    pl.semaphore_wait(barrier, n - 1)
+
+
+def fetch_kernel(
+    n, wanted_ref, planes_ref, tiles_ref, asked_ref,
+    asking, spread, own, outgoing, ask_send, ask_recv, tile_send, tile_recv,
+):
+    me = lax.axis_index("tile")
+    tiles_dev = planes_ref.shape[1]
+    pieces = planes_ref.shape[2] // BLK
+
+    def fill(o, carry):
+        for p in range(3):
+            asking[o, p : p + 1, :] = jnp.full((1, BLK), wanted_ref[p * n + o], jnp.int32).astype(F32)
+        return carry
+
+    asking[...] = jnp.zeros_like(asking)
+    lax.fori_loop(0, n, fill, 0)
+    enter(n)
+
+    def ask(d):
+        to = lax.rem(me + d, n)
+        return pltpu.make_async_remote_copy(
+            src_ref=asking.at[to], dst_ref=asked_ref.at[me], send_sem=ask_send.at[d], recv_sem=ask_recv.at[d],
+            device_id=peer(d, n), device_id_type=pl.DeviceIdType.MESH,
+        )
+
+    def asked_by(d):
+        source = lax.rem(me - d + n, n)
+        return pltpu.make_async_remote_copy(
+            src_ref=asking.at[source], dst_ref=asked_ref.at[source], send_sem=ask_send.at[d],
+            recv_sem=ask_recv.at[d], device_id=peer(d, n), device_id_type=pl.DeviceIdType.MESH,
+        )
+
+    def give(d):
+        to = lax.rem(me - d + n, n)
+        return pltpu.make_async_remote_copy(
+            src_ref=outgoing.at[to], dst_ref=tiles_ref.at[me], send_sem=tile_send.at[d],
+            recv_sem=tile_recv.at[d], device_id=peer(n - d, n), device_id_type=pl.DeviceIdType.MESH,
+        )
+
+    def given_by(d):
+        source = lax.rem(me + d, n)
+        return pltpu.make_async_remote_copy(
+            src_ref=outgoing.at[source], dst_ref=tiles_ref.at[source], send_sem=tile_send.at[d],
+            recv_sem=tile_recv.at[d], device_id=peer(n - d, n), device_id_type=pl.DeviceIdType.MESH,
+        )
+
+    def start_ask(d, carry):
+        ask(d).start()
+        return carry
+
+    lax.fori_loop(1, n, start_ask, 0)
+    asked_ref[me] = asking[me]
+    for p in range(3):
+        wide = planes_ref[p].astype(F32)
+        for i in range(pieces):
+            spread[p, :, i, :] = wide[:, i * BLK : (i + 1) * BLK]
+    own[...] = spread[...].astype(BF16)
+
+    def choose(source, p):
+        want = jnp.broadcast_to(asked_ref[source, p : p + 1, :], (pieces, BLK)).astype(BF16)
+        got = jnp.zeros((pieces, BLK), BF16)
+        for k in range(tiles_dev):
+            got = jnp.where(want == jnp.asarray(k, BF16), own[p, k], got)
+        return got
+
+    def serve(d, carry):
+        asked_by(d).wait_recv()
+        to = lax.rem(me - d + n, n)
+        for p in range(3):
+            outgoing[to, p] = choose(to, p)
+        give(d).start()
+        return carry
+
+    lax.fori_loop(1, n, serve, 0)
+    for p in range(3):
+        tiles_ref[me, p] = choose(me, p)
+
+    def finish(d, carry):
+        ask(d).wait_send()
+        give(d).wait_send()
+        given_by(d).wait_recv()
+        return carry
+
+    lax.fori_loop(1, n, finish, 0)
+
+
+def fetch(wanted, planes, n):
+    pieces = planes.shape[2] // BLK
+    tiles_dev = planes.shape[1]
+    vmem = pl.BlockSpec(memory_space=pltpu.VMEM)
+    return pl.pallas_call(
+        functools.partial(fetch_kernel, n),
+        out_shape=(
+            jax.ShapeDtypeStruct((n, 3, pieces, BLK), BF16),
+            jax.ShapeDtypeStruct((n, 8, BLK), F32),
+        ),
+        in_specs=[pl.BlockSpec(memory_space=pltpu.SMEM), vmem],
+        out_specs=(vmem, vmem),
+        scratch_shapes=[
+            pltpu.VMEM((n, 8, BLK), F32),
+            pltpu.VMEM((3, tiles_dev, pieces, BLK), F32),
+            pltpu.VMEM((3, tiles_dev, pieces, BLK), BF16),
+            pltpu.VMEM((n, 3, pieces, BLK), BF16),
+        ]
+        + [pltpu.SemaphoreType.DMA((n,))] * 4,
+        compiler_params=pltpu.CompilerParams(
+            collective_id=0, has_side_effects=True, vmem_limit_bytes=24 * 1024 * 1024
+        ),
+        name="fetch_tiles",
+    )(wanted, planes)
+
+
+def give_back_kernel(n, sums_ref, asked_ref, out_ref, outgoing, landed, total, send_sem, recv_sem):
+    me = lax.axis_index("tile")
+    tiles_dev = out_ref.shape[1]
+    pieces = out_ref.shape[2] // BLK
+
+    def fill(o, carry):
+        outgoing[o] = sums_ref[o].astype(BF16)
+        return carry
+
+    lax.fori_loop(0, n, fill, 0)
+    enter(n)
+
+    def give(d):
+        to = lax.rem(me + d, n)
+        return pltpu.make_async_remote_copy(
+            src_ref=outgoing.at[to], dst_ref=landed.at[me], send_sem=send_sem.at[d], recv_sem=recv_sem.at[d],
+            device_id=peer(d, n), device_id_type=pl.DeviceIdType.MESH,
+        )
+
+    def given_by(d):
+        source = lax.rem(me - d + n, n)
+        return pltpu.make_async_remote_copy(
+            src_ref=outgoing.at[source], dst_ref=landed.at[source], send_sem=send_sem.at[d],
+            recv_sem=recv_sem.at[d], device_id=peer(d, n), device_id_type=pl.DeviceIdType.MESH,
+        )
+
+    def start(d, carry):
+        give(d).start()
+        return carry
+
+    lax.fori_loop(1, n, start, 0)
+
+    for p in range(3):
+        mine = sums_ref[me, p]
+        want = jnp.broadcast_to(asked_ref[me, p : p + 1, :], (pieces, BLK))
+        for k in range(tiles_dev):
+            total[p, k] = jnp.where(want == k, mine, 0.0)
+
+    def add(d, carry):
+        given_by(d).wait_recv()
+        source = lax.rem(me - d + n, n)
+        for p in range(3):
+            came = landed[source, p].astype(F32)
+            want = jnp.broadcast_to(asked_ref[source, p : p + 1, :], (pieces, BLK))
+            for k in range(tiles_dev):
+                total[p, k] += jnp.where(want == k, came, 0.0)
+        return carry
+
+    lax.fori_loop(1, n, add, 0)
+    for p in range(3):
+        for i in range(pieces):
+            out_ref[p, :, i * BLK : (i + 1) * BLK] = total[p, :, i, :]
+
+    def finish(d, carry):
+        give(d).wait_send()
+        return carry
+
+    lax.fori_loop(1, n, finish, 0)
+
+
+def give_back(sums, asked, tiles_dev, n):
+    pieces = sums.shape[2]
+    vmem = pl.BlockSpec(memory_space=pltpu.VMEM)
+    return pl.pallas_call(
+        functools.partial(give_back_kernel, n),
+        out_shape=jax.ShapeDtypeStruct((3, tiles_dev, pieces * BLK), F32),
+        in_specs=[vmem, vmem],
+        out_specs=vmem,
+        scratch_shapes=[
+            pltpu.VMEM((n, 3, pieces, BLK), BF16),
+            pltpu.VMEM((n, 3, pieces, BLK), BF16),
+            pltpu.VMEM((3, tiles_dev, pieces, BLK), F32),
+            pltpu.SemaphoreType.DMA((n,)),
+            pltpu.SemaphoreType.DMA((n,)),
+        ],
+        compiler_params=pltpu.CompilerParams(
+            collective_id=1, has_side_effects=True, vmem_limit_bytes=24 * 1024 * 1024
+        ),
+        name="give_back",
+    )(sums, asked)
+
+
 def shards(planes, decoder_in, decoder_out, corner, fraction, block_slot, wanted, ray_id, ray_grad):
     owners = lax.axis_size("tile")
-    tiles_dev = planes.shape[1]
-    row_len = planes.shape[2]
-    per_owner = wanted.shape[3]
-    slot_count = owners * per_owner
-    served = lax.all_to_all(wanted, "tile", split_axis=2, concat_axis=0, tiled=True)
-    served = jnp.transpose(served[:, :, 0, :], (1, 0, 2))
-    local_ids = jnp.arange(tiles_dev, dtype=jnp.int32)
-    serve_pick = (served[..., None] == local_ids).astype(BF16)
-    outgoing = jnp.einsum(
-        "pock,pkf->pocf", serve_pick, planes, preferred_element_type=F32
-    ).astype(BF16)
-    incoming = lax.all_to_all(outgoing, "tile", split_axis=1, concat_axis=1, tiled=True)
-    tiles = incoming.reshape(3, slot_count, row_len // BLK, BLK)
+    tiles, asked = fetch(wanted.reshape(-1), planes, owners)
     slot_sums = compute(block_slot, tiles, decoder_in, decoder_out, ray_grad[0], corner, fraction, ray_id)
-    returned = lax.all_to_all(
-        slot_sums.reshape(3, owners, per_owner, row_len).astype(BF16),
-        "tile",
-        split_axis=1,
-        concat_axis=1,
-        tiled=True,
-    )
-    returned = returned.reshape(3, slot_count, row_len)
-    local_places = jnp.arange(tiles_dev, dtype=jnp.int32)[None, :, None]
-    owner_pick = (local_places == served.reshape(3, 1, slot_count)).astype(BF16)
-    return jnp.einsum("pts,psf->ptf", owner_pick, returned, preferred_element_type=F32)
+    return give_back(slot_sums, asked, planes.shape[1], owners)
 
 
 def solution(mesh):

time: 102 us -> 89.9 us (0.88)
  Pallas kernels: 55.4 us -> 79.7 us
  waiting for transfers between devices: 14 us -> 0 us
  blocking collectives: 12.8 us -> 0 us
  starting transfers between devices: 10.9 us -> 0 us
  local copies, waits for them, and re-layouts: 5.84 us -> 8.27 us
  matrix products: 1.26 us -> 0 us
    pallas_call x0 -> x2, Pallas kernels: none -> 24.3 us  [the longest x1 16.5 us: fetch(): pl.pallas_call(functools.partial(fetch_kernel, n), out_shape=(jax.ShapeDt...]
    all_to_all x2 -> x0, waiting for transfers between devices: 14 us -> none  [the longest x1 9.19 us: shards(): lax.all_to_all(outgoing, 'tile', split_axis=1, concat_axis=1, tiled=True)]
    all_to_all x1 -> x0, blocking collectives: 12.8 us -> none  [shards(): lax.all_to_all(slot_sums.reshape(3, owners, per_owner, row_len).astype(BF...]
    all_to_all x2 -> x0, starting transfers between devices: 10.9 us -> none  [the longest x1 7.39 us: shards(): lax.all_to_all(wanted, 'tile', split_axis=2, concat_axis=0, tiled=True)]
    unnamed x14 -> x13, local copies, waits for them, and re-layouts: 2.74 us -> 6.53 us
    dot_general x2 -> x0, matrix products: 1.26 us -> none  [the longest x1 1 us: shards(): jnp.einsum('pts,psf->ptf', owner_pick, returned, preferred_element_type=F32)]
    convert_element_type x3 -> x0, local copies, waits for them, and re-layouts: 1.13 us -> none  [the longest x1 0.87 us: shards(): outgoing = jnp.einsum('pock,pkf->pocf', serve_pick, planes, preferred_ele...]
  transfers between devices with their start and end apart: 2 -> 0, of which waited for: 2 -> 0; matrix products, arithmetic and copies ran while one was open for 2% -> 0% of each run, Pallas kernels for 0% -> 0%
where the time goes in v2:
time: 89.9 us; the launch traced here: 89.4 us
  Pallas kernels  79.7 us (89%)
  local copies, waits for them, and re-layouts  8.27 us (9%)
  other arithmetic  1.41 us (2%)
    pallas_call x1, Pallas kernels, compute(): pl.pallas_call(compute_kernel, grid_spec=grid_spec, out_shape=jax.ShapeDt...  55.4 us
    pallas_call x1, Pallas kernels, fetch(): pl.pallas_call(functools.partial(fetch_kernel, n), out_shape=(jax.ShapeDt...  16.5 us
    pallas_call x1, Pallas kernels, give_back(): pl.pallas_call(functools.partial(give_back_kernel, n), out_shape=jax.Shap...  7.74 us
    unnamed x13, local copies, waits for them, and re-layouts  6.53 us

profile of v2, /device:TPU:0, one launch (start us, length us, event | category | flops | bytes accessed | tf_op | source)
XLA Modules:
  0.0 89.4 jit_solution(13664490049379642364)
XLA Ops:
  0.0 0.7 multiply_convert_fusion.1
  0.7 0.7 reduce
  1.4 0.1 reshape.6.wanted_ref
  1.5 0.7 slice.7
  2.2 0.7 slice.6
  2.9 0.1 copy.16.win_t_ref
  3.0 0.1 copy.17.wout_ref
  3.1 0.0 copy-start.3
  3.2 0.9 copy-done.3
  4.1 16.5 %fetch_tiles.1 = (bf16[16,3,16,128]{3,2,1,0:T(8,128)(2,1)S(1)}, f32[16,8,128]{2,1,0:T(8,128)S(1)}) custom-call(s32[48]{0:T(128)S(1)} %reshape.6.wanted_ref, bf16[3,8,2048]{2,1,0:T(8,128)(2,1)S(1)} %copy-done.3), custom_call_target="tpu_custom_call" | custom-call | tf_op jit(solution)/shard_map/fetch_tiles/pallas_call | solution.py:256
  20.6 0.0 copy-start
  20.6 1.4 %copy-done = f32[3,2,65536]{2,1,0:T(2,128)S(1)} copy-done((f32[3,2,65536]{2,1,0:T(2,128)S(1)}, f32[3,2,65536]{2,1,0:T(2,128)}, u32[]{:S(2)}) %copy-start) | copy-done | bytes 1572888
  22.0 0.0 copy-start.1
  22.0 1.2 %copy-done.1 = s32[3,65536]{1,0:T(4,128)S(1)} copy-done((s32[3,65536]{1,0:T(4,128)S(1)}, s32[3,65536]{1,0:T(4,128)}, u32[]{:S(2)}) %copy-start.1) | copy-done | bytes 786456
  23.2 0.0 copy-start.2
  23.2 0.9 %copy-done.2 = s32[1,65536]{1,0:T(1,128)S(1)} copy-done((s32[1,65536]{1,0:T(1,128)S(1)}, s32[1,65536]{1,0:T(1,128)}, u32[]{:S(2)}) %copy-start.2) | copy-done | bytes 262168
  24.2 0.0 copy-start.4
  24.2 0.7 copy-done.4
  24.9 0.0 copy-start.5
  24.9 0.7 copy-done.5
  25.6 55.4 %field_grad.1.sums_ref = f32[16,3,16,128]{3,2,1,0:T(8,128)S(1)} custom-call(s32[3,512]{1,0:T(4,128)S(1)} %copy-done.4, bf16[16,3,16,128]{3,2,1,0:T(8,128)(2,1)S(1)} %get-tuple-element.7.tiles_ref, bf16[64,32]{1,0:T(8,128)(2,1)S(1)} %copy.16.win_t_ref, bf16[32,64]{1,0:T(8,128)(2,1)S(1)} %fusion.win_ref, bf16[64,8]{1,0:T(8,128)(2,1)S(1)} %copy.17.wout_ref, ...), custom_call_target="tpu_custom_call" | custom-call | tf_op jit(solution)/shard_map/field_grad/pallas_call | solution.py:143
  81.0 7.7 %give_back.1 = f32[3,8,2048]{2,1,0:T(8,128)S(1)} custom-call(f32[16,3,16,128]{3,2,1,0:T(8,128)S(1)} %field_grad.1.sums_ref, f32[16,8,128]{2,1,0:T(8,128)S(1)} %get-tuple-element.8.asked_ref), custom_call_target="tpu_custom_call" | custom-call | tf_op jit(solution)/shard_map/give_back/pallas_call | solution.py:341
  88.8 0.7 copy.19
  (3 shorter events, 0.0 us)
Async XLA Ops:
  3.1 0.9 %copy-start.3 = (bf16[3,8,2048]{2,1,0:T(8,128)(2,1)S(1)}, bf16[3,8,2048]{2,1,0:T(8,128)(2,1)}, u32[]{:S(2)}) copy-start(bf16[3,8,2048]{2,1,0:T(8,128)(2,1)} %planes_ref.1) | copy-start | bytes 294916
  20.6 1.4 %copy-start = (f32[3,2,65536]{2,1,0:T(2,128)S(1)}, f32[3,2,65536]{2,1,0:T(2,128)}, u32[]{:S(2)}) copy-start(f32[3,2,65536]{2,1,0:T(2,128)} %fraction_ref.1) | copy-start | bytes 4718596
  22.0 1.2 %copy-start.1 = (s32[3,65536]{1,0:T(4,128)S(1)}, s32[3,65536]{1,0:T(4,128)}, u32[]{:S(2)}) copy-start(s32[3,65536]{1,0:T(4,128)} %corner_ref.1) | copy-start | bytes 2359300
  23.2 0.9 %copy-start.2 = (s32[1,65536]{1,0:T(1,128)S(1)}, s32[1,65536]{1,0:T(1,128)}, u32[]{:S(2)}) copy-start(s32[1,65536]{1,0:T(1,128)} %ray_ref.1) | copy-start | bytes 786436
  24.2 0.7 copy-start.4
  24.9 0.7 copy-start.5

commit v3 on v2

--- a/solution.py
+++ b/solution.py
@@ -11,8 +11,7 @@
 TS = 8
 BLK = 128
 CHUNK = 8192
-GROUP = 16
-UNROLL = 1
+GROUP = 32
 
 F32 = jnp.float32
 BF16 = jnp.bfloat16
@@ -48,81 +47,102 @@
 
 
 def compute_kernel(
-    slots_ref, tiles_ref, win_t_ref, win_ref, wout_ref, table_ref, corner_ref, fraction_ref, ray_ref, acc_ref
+    slots_ref, tiles_ref, win_ref, wout_ref, grad_ref, corner_ref, fraction_ref, ray_ref, acc_ref,
+    win_t, win, wout, table, *sums
 ):
     step = pl.program_id(0)
+    halves = table.shape[0]
+    channels = win_ref.shape[0]
+    half_c = channels // 2
 
     @pl.when(step == 0)
     def _():
-        acc_ref[...] = jnp.zeros_like(acc_ref)
-
-    halves = table_ref.shape[0]
+        for one in sums:
+            one[...] = jnp.zeros_like(one)
+        by_parity = jnp.concatenate(
+            [win_ref[pl.ds(0, half_c, stride=2), :], win_ref[pl.ds(1, half_c, stride=2), :]], axis=0
+        )
+        win[...] = by_parity.astype(BF16)
+        win_t[...] = (by_parity.T * 0.5).astype(BF16)
+        out_at = lax.broadcasted_iota(jnp.int32, (OUTS, 2 * OUTS * halves), 0)
+        copy_at = lax.broadcasted_iota(jnp.int32, (OUTS, 2 * OUTS * halves), 1) % OUTS
+        repeat = jnp.where(out_at == copy_at, 0.5, 0.0).astype(BF16)
+        wout[...] = dot(wout_ref[...].astype(BF16), repeat).astype(BF16)
+        for h in range(halves):
+            for k in range(2):
+                first = (2 * h + k) * BLK
+                table[h, k * OUTS : (k + 1) * OUTS, :] = grad_ref[0, :, first : first + BLK]
+
     blocks = CHUNK // BLK
-
-    @functools.partial(lax.fori_loop, 0, blocks // GROUP, init_val=None, unroll=UNROLL)
-    def _(at, carry):
-        wide, feats, slots = [], [], []
-        grads_out = []
+    rows = table.shape[1]
+
+    def body(at, carry):
+        slots = [
+            [slots_ref[p, step * blocks + at * GROUP + b] for p in range(3)] for b in range(GROUP)
+        ]
+        lanes = [
+            pl.ds(pl.multiple_of((at * GROUP + b) * BLK, BLK), BLK) for b in range(GROUP)
+        ]
+        wide, grads_out = [], []
+        feats = [[None] * 3 for b in range(GROUP)]
         for b in range(GROUP):
-            local = at * GROUP + b
-            lanes = pl.ds(pl.multiple_of(local * BLK, BLK), BLK)
-            wides, fs, ss = [], [], []
+            wides = []
             for p in range(3):
-                slot = slots_ref[p, step * blocks + local]
                 m = cell_weights(
-                    corner_ref[p : p + 1, lanes], fraction_ref[p, 0:1, lanes], fraction_ref[p, 1:2, lanes]
+                    corner_ref[p : p + 1, lanes[b]],
+                    fraction_ref[p, 0:1, lanes[b]],
+                    fraction_ref[p, 1:2, lanes[b]],
                 )
                 z = jnp.zeros_like(m)
                 w = jnp.concatenate(
                     [jnp.concatenate([m, z], axis=1), jnp.concatenate([z, m], axis=1)], axis=0
                 )
-                f = dot(tiles_ref[slot, p], w)
-                fs.append(jnp.concatenate([f[:, :BLK], f[:, BLK:]], axis=0))
-                wides.append(w)
-                ss.append(slot)
+                wides.append(m)
+                f = dot(tiles_ref[slots[b][p], p], w)
+                feats[b][p] = jnp.concatenate([f[:, :BLK], f[:, BLK:]], axis=0)
             wide.append(wides)
-            feats.append(fs)
-            slots.append(ss)
-            ray = ray_ref[0:1, lanes]
-            rows = table_ref.shape[1]
+            ray = ray_ref[0:1, lanes[b]]
             picks = []
             idx = jnp.broadcast_to(ray & (BLK - 1), (rows, BLK))
-            half = jnp.broadcast_to(ray >> 7, (rows, BLK))
+            part = jnp.broadcast_to(ray >> 7, (rows, BLK))
             sub = lax.broadcasted_iota(jnp.int32, (rows, BLK), 0) // OUTS
             for h in range(halves):
-                got = jnp.take_along_axis(table_ref[h], idx, axis=1)
-                picks.append(jnp.where(half == sub + 2 * h, got, 0.0))
+                got = jnp.take_along_axis(table[h], idx, axis=1)
+                picks.append(jnp.where(part == sub + 2 * h, got, 0.0))
             grads_out.append(jnp.concatenate(picks, axis=0))
         f = [jnp.concatenate([feats[b][p] for b in range(GROUP)], axis=1) for p in range(3)]
         others = [f[1] * f[2], f[0] * f[2], f[0] * f[1]]
         product = (others[2] * f[2]).astype(BF16)
         grads_out = jnp.concatenate(grads_out, axis=1).astype(BF16)
-        half_pre = dot(win_t_ref[...], product)
-        hidden = dot(wout_ref[...], grads_out)
+        half_pre = dot(win_t[...], product)
+        hidden = dot(wout[...], grads_out)
         t = jnp.tanh(half_pre)
         pre_grad = hidden * ((1.0 + t) * (1.0 + half_pre * (1.0 - t)))
-        prod_grad = dot(win_ref[...], pre_grad.astype(BF16))
+        prod_grad = dot(win[...], pre_grad.astype(BF16))
         for p in range(3):
             fg = (prod_grad * others[p]).astype(BF16)
-            half_c = fg.shape[0] // 2
             for b in range(GROUP):
-                part = fg[:, b * BLK : (b + 1) * BLK]
-                lhs = jnp.concatenate([part[:half_c], part[half_c:]], axis=1)
-                slot = slots[b][p]
-                acc_ref[slot, p] += dot_t(lhs, wide[b][p])
-        return carry
-
-
-def compute(slots, tiles, decoder_in, decoder_out, ray_table, corner, fraction, ray_id):
+                piece = fg[:, b * BLK : (b + 1) * BLK]
+                sums[p][slots[b][p]] += dot_t(piece, wide[b][p])
+        return carry
+
+    lax.fori_loop(0, blocks // GROUP, body, 0)
+
+    @pl.when(step == pl.num_programs(0) - 1)
+    def _():
+        for p in range(3):
+            def put(k, carry):
+                one = sums[p][k]
+                acc_ref[k, p] = jnp.concatenate([one[:half_c], one[half_c:]], axis=1).astype(acc_ref.dtype)
+                return carry
+
+            lax.fori_loop(0, acc_ref.shape[0], put, 0)
+
+
+def compute(slots, tiles, decoder_in, decoder_out, ray_grad, corner, fraction, ray_id):
     channels, hid = decoder_in.shape
     samples = corner.shape[1]
-    rays = ray_table.shape[1]
-    by_parity = jnp.concatenate([decoder_in[0::2], decoder_in[1::2]], axis=0)
-    win_t = (by_parity.T * 0.5).astype(BF16)
-    win = by_parity.astype(BF16)
-    halves = rays // (2 * BLK)
-    wout = jnp.concatenate([decoder_out * 0.5] * (2 * halves), axis=1).astype(BF16)
-    table = ray_table.reshape(OUTS, halves, 2, BLK).transpose(1, 2, 0, 3).reshape(halves, 2 * OUTS, BLK)
+    halves = ray_grad.shape[2] // (2 * BLK)
     steps = samples // CHUNK
     vmem = pl.BlockSpec(memory_space=pltpu.VMEM)
     grid_spec = pltpu.PrefetchScalarGridSpec(
@@ -133,20 +153,26 @@
             vmem,
             vmem,
             vmem,
-            vmem,
             pl.BlockSpec((3, CHUNK), lambda i, s: (0, i)),
             pl.BlockSpec((3, 2, CHUNK), lambda i, s: (0, 0, i)),
             pl.BlockSpec((1, CHUNK), lambda i, s: (0, i)),
         ],
         out_specs=pl.BlockSpec(tiles.shape, lambda i, s: (0, 0, 0, 0)),
+        scratch_shapes=[
+            pltpu.VMEM((hid, channels), BF16),
+            pltpu.VMEM((channels, hid), BF16),
+            pltpu.VMEM((hid, 2 * OUTS * halves), BF16),
+            pltpu.VMEM((halves, 2 * OUTS, BLK), F32),
+        ]
+        + [pltpu.VMEM((tiles.shape[0],) + (channels, TS * TS), F32)] * 3,
     )
     return pl.pallas_call(
         compute_kernel,
         grid_spec=grid_spec,
-        out_shape=jax.ShapeDtypeStruct(tiles.shape, F32),
-        compiler_params=pltpu.CompilerParams(vmem_limit_bytes=48 * 1024 * 1024),
+        out_shape=jax.ShapeDtypeStruct(tiles.shape, BF16),
+        compiler_params=pltpu.CompilerParams(vmem_limit_bytes=60 * 1024 * 1024),
         name="field_grad",
-    )(slots, tiles, win_t, win, wout, table, corner, fraction, ray_id)
+    )(slots, tiles, decoder_in, decoder_out, ray_grad, corner, fraction, ray_id)
 
 
 def peer(d, n):
@@ -275,29 +301,24 @@
     )(wanted, planes)
 
 
-def give_back_kernel(n, sums_ref, asked_ref, out_ref, outgoing, landed, total, send_sem, recv_sem):
+def give_back_kernel(n, sums_ref, asked_ref, out_ref, landed, total, send_sem, recv_sem):
     me = lax.axis_index("tile")
     tiles_dev = out_ref.shape[1]
     pieces = out_ref.shape[2] // BLK
 
-    def fill(o, carry):
-        outgoing[o] = sums_ref[o].astype(BF16)
-        return carry
-
-    lax.fori_loop(0, n, fill, 0)
     enter(n)
 
     def give(d):
         to = lax.rem(me + d, n)
         return pltpu.make_async_remote_copy(
-            src_ref=outgoing.at[to], dst_ref=landed.at[me], send_sem=send_sem.at[d], recv_sem=recv_sem.at[d],
+            src_ref=sums_ref.at[to], dst_ref=landed.at[me], send_sem=send_sem.at[d], recv_sem=recv_sem.at[d],
             device_id=peer(d, n), device_id_type=pl.DeviceIdType.MESH,
         )
 
     def given_by(d):
         source = lax.rem(me - d + n, n)
         return pltpu.make_async_remote_copy(
-            src_ref=outgoing.at[source], dst_ref=landed.at[source], send_sem=send_sem.at[d],
+            src_ref=sums_ref.at[source], dst_ref=landed.at[source], send_sem=send_sem.at[d],
             recv_sem=recv_sem.at[d], device_id=peer(d, n), device_id_type=pl.DeviceIdType.MESH,
         )
 
@@ -308,7 +329,7 @@
     lax.fori_loop(1, n, start, 0)
 
     for p in range(3):
-        mine = sums_ref[me, p]
+        mine = sums_ref[me, p].astype(F32)
         want = jnp.broadcast_to(asked_ref[me, p : p + 1, :], (pieces, BLK))
         for k in range(tiles_dev):
             total[p, k] = jnp.where(want == k, mine, 0.0)
@@ -345,7 +366,6 @@
         out_specs=vmem,
         scratch_shapes=[
             pltpu.VMEM((n, 3, pieces, BLK), BF16),
-            pltpu.VMEM((n, 3, pieces, BLK), BF16),
             pltpu.VMEM((3, tiles_dev, pieces, BLK), F32),
             pltpu.SemaphoreType.DMA((n,)),
             pltpu.SemaphoreType.DMA((n,)),
@@ -360,7 +380,7 @@
 def shards(planes, decoder_in, decoder_out, corner, fraction, block_slot, wanted, ray_id, ray_grad):
     owners = lax.axis_size("tile")
     tiles, asked = fetch(wanted.reshape(-1), planes, owners)
-    slot_sums = compute(block_slot, tiles, decoder_in, decoder_out, ray_grad[0], corner, fraction, ray_id)
+    slot_sums = compute(block_slot, tiles, decoder_in, decoder_out, ray_grad, corner, fraction, ray_id)
     return give_back(slot_sums, asked, planes.shape[1], owners)
 
 

time: 89.9 us -> 71.9 us (0.80)
  Pallas kernels: 79.7 us -> 66.2 us
  local copies, waits for them, and re-layouts: 8.27 us -> 4.63 us
    pallas_call x1, Pallas kernels: 55.4 us -> 42.3 us  [compute(): pl.pallas_call(compute_kernel, grid_spec=grid_spec, out_shape=jax.ShapeDt...]
    unnamed x13 -> x8, local copies, waits for them, and re-layouts: 6.53 us -> 4.55 us
    slice x2 -> x0, local copies, waits for them, and re-layouts: 1.45 us -> none  [compute(): by_parity = jnp.concatenate([decoder_in[0::2], decoder_in[1::2]], axis=0)]
where the time goes in v3:
time: 71.9 us; the launch traced here: 71.6 us
  Pallas kernels  66.2 us (92%)
  local copies, waits for them, and re-layouts  4.63 us (6%)
    pallas_call x1, Pallas kernels, compute(): pl.pallas_call(compute_kernel, grid_spec=grid_spec, out_shape=jax.ShapeDt...  42.3 us
    pallas_call x1, Pallas kernels, fetch(): pl.pallas_call(functools.partial(fetch_kernel, n), out_shape=(jax.ShapeDt...  16.5 us
    pallas_call x1, Pallas kernels, give_back(): pl.pallas_call(functools.partial(give_back_kernel, n), out_shape=jax.Shap...  7.37 us
    unnamed x8, local copies, waits for them, and re-layouts  4.55 us

profile of v3, /device:TPU:0, one launch (start us, length us, event | category | flops | bytes accessed | tf_op | source)
XLA Modules:
  0.0 71.6 jit_solution(16803396385463032153)
XLA Ops:
  0.0 0.7 reduce
  0.7 0.1 reshape.3.wanted_ref
  0.8 1.4 %copy.10.wout_ref = f32[64,4]{1,0:T(8,128)} copy(f32[64,4]{0,1:T(4,128)} %param.11) | data formatting | bytes 2048 | tf_op args[2]
  2.2 0.0 copy-start.2
  2.2 0.9 %copy-done.2 = bf16[3,8,2048]{2,1,0:T(8,128)(2,1)S(1)} copy-done((bf16[3,8,2048]{2,1,0:T(8,128)(2,1)S(1)}, bf16[3,8,2048]{2,1,0:T(8,128)(2,1)}, u32[]{:S(2)}) %copy-start.2) | copy-done | bytes 98328
  3.1 16.5 %fetch_tiles.1 = (bf16[16,3,16,128]{3,2,1,0:T(8,128)(2,1)S(1)}, f32[16,8,128]{2,1,0:T(8,128)S(1)}) custom-call(s32[48]{0:T(128)S(1)} %reshape.3.wanted_ref, bf16[3,8,2048]{2,1,0:T(8,128)(2,1)S(1)} %copy-done.2), custom_call_target="tpu_custom_call" | custom-call | tf_op jit(solution)/shard_map/fetch_tiles/pallas_call | solution.py:282
  19.6 0.0 copy-start.1
  19.6 0.7 copy-done.1
  20.3 42.3 %field_grad.1.sums_ref = bf16[16,3,16,128]{3,2,1,0:T(8,128)(2,1)} custom-call(s32[3,512]{1,0:T(4,128)} %slots_ref.1, bf16[16,3,16,128]{3,2,1,0:T(8,128)(2,1)} %copy-done.1, f32[32,64]{1,0:T(8,128)} %win_ref.1, f32[64,4]{1,0:T(8,128)} %copy.10.wout_ref, f32[1,4,256]{2,1,0:T(4,128)} %grad_ref.1, s32[3,65536]{1,0:T(4,128)} %corner_ref.1, ...), custom_call_target="tpu_custom_call" | custom-call | tf_op jit(solution)/shard_map/field_grad/pallas_call | solution.py:169
  62.6 0.0 copy-start
  62.6 0.9 %copy-done = bf16[16,3,16,128]{3,2,1,0:T(8,128)(2,1)S(1)} copy-done((bf16[16,3,16,128]{3,2,1,0:T(8,128)(2,1)S(1)}, bf16[16,3,16,128]{3,2,1,0:T(8,128)(2,1)}, u32[]{:S(2)}) %copy-start) | copy-done | bytes 196632
  63.5 7.4 %give_back.1 = f32[3,8,2048]{2,1,0:T(8,128)S(1)} custom-call(bf16[16,3,16,128]{3,2,1,0:T(8,128)(2,1)S(1)} %copy-done, f32[16,8,128]{2,1,0:T(8,128)S(1)} %get-tuple-element.8.asked_ref), custom_call_target="tpu_custom_call" | custom-call | tf_op jit(solution)/shard_map/give_back/pallas_call | solution.py:362
  70.9 0.7 copy.12
Async XLA Ops:
  2.2 0.9 %copy-start.2 = (bf16[3,8,2048]{2,1,0:T(8,128)(2,1)S(1)}, bf16[3,8,2048]{2,1,0:T(8,128)(2,1)}, u32[]{:S(2)}) copy-start(bf16[3,8,2048]{2,1,0:T(8,128)(2,1)} %planes_ref.1) | copy-start | bytes 294916
  19.6 0.7 copy-start.1
  62.6 0.9 %copy-start = (bf16[16,3,16,128]{3,2,1,0:T(8,128)(2,1)S(1)}, bf16[16,3,16,128]{3,2,1,0:T(8,128)(2,1)}, u32[]{:S(2)}) copy-start(bf16[16,3,16,128]{3,2,1,0:T(8,128)(2,1)} %field_grad.1.sums_ref) | copy-start | bytes 589828

commit v4 on v3

--- a/solution.py
+++ b/solution.py
@@ -10,8 +10,8 @@
 OUTS = 4
 TS = 8
 BLK = 128
-CHUNK = 8192
-GROUP = 32
+CHUNK = 16384
+GROUP = 64
 
 F32 = jnp.float32
 BF16 = jnp.bfloat16
@@ -67,7 +67,9 @@
         out_at = lax.broadcasted_iota(jnp.int32, (OUTS, 2 * OUTS * halves), 0)
         copy_at = lax.broadcasted_iota(jnp.int32, (OUTS, 2 * OUTS * halves), 1) % OUTS
         repeat = jnp.where(out_at == copy_at, 0.5, 0.0).astype(BF16)
-        wout[...] = dot(wout_ref[...].astype(BF16), repeat).astype(BF16)
+        wout[...] = lax.dot_general(
+            wout_ref[...].astype(BF16), repeat, (((0,), (0,)), ((), ())), preferred_element_type=F32
+        ).astype(BF16)
         for h in range(halves):
             for k in range(2):
                 first = (2 * h + k) * BLK
@@ -172,7 +174,7 @@
         out_shape=jax.ShapeDtypeStruct(tiles.shape, BF16),
         compiler_params=pltpu.CompilerParams(vmem_limit_bytes=60 * 1024 * 1024),
         name="field_grad",
-    )(slots, tiles, decoder_in, decoder_out, ray_grad, corner, fraction, ray_id)
+    )(slots, tiles, decoder_in, decoder_out.T, ray_grad, corner, fraction, ray_id)
 
 
 def peer(d, n):

time: 71.9 us -> 69.8 us (0.971)
  local copies, waits for them, and re-layouts: 4.63 us -> 3.26 us
    unnamed x8 -> x7, local copies, waits for them, and re-layouts: 4.55 us -> 3.17 us
where the time goes in v4:
time: 69.8 us; the launch traced here: 69.6 us
  Pallas kernels  65.6 us (94%)
  local copies, waits for them, and re-layouts  3.26 us (5%)
  other arithmetic  0.7 us (1%)
    pallas_call x1, Pallas kernels, compute(): pl.pallas_call(compute_kernel, grid_spec=grid_spec, out_shape=jax.ShapeDt...  41.7 us
    pallas_call x1, Pallas kernels, fetch(): pl.pallas_call(functools.partial(fetch_kernel, n), out_shape=(jax.ShapeDt...  16.5 us
    pallas_call x1, Pallas kernels, give_back(): pl.pallas_call(functools.partial(give_back_kernel, n), out_shape=jax.Shap...  7.37 us
    unnamed x7, local copies, waits for them, and re-layouts  3.17 us

profile of v4, /device:TPU:0, one launch (start us, length us, event | category | flops | bytes accessed | tf_op | source)
XLA Modules:
  0.0 69.6 jit_solution(8515321008991353141)
XLA Ops:
  0.0 0.7 %reduce = s32[3,16]{1,0:T(4,128)S(1)} reduce(s32[1,3,16,1]{2,3,1,0:T(1,128)} %param.15, s32[]{:T(128)} %constant.4), dimensions={0,3}, to_apply=%param.15.reduce_sub_computation | reduce | bytes 388 | tf_op args[6]
  0.7 0.1 reshape.3.wanted_ref
  0.8 0.0 copy-start.2
  0.8 0.9 %copy-done.2 = bf16[3,8,2048]{2,1,0:T(8,128)(2,1)S(1)} copy-done((bf16[3,8,2048]{2,1,0:T(8,128)(2,1)S(1)}, bf16[3,8,2048]{2,1,0:T(8,128)(2,1)}, u32[]{:S(2)}) %copy-start.2) | copy-done | bytes 98328
  1.7 16.5 %fetch_tiles.1 = (bf16[16,3,16,128]{3,2,1,0:T(8,128)(2,1)S(1)}, f32[16,8,128]{2,1,0:T(8,128)S(1)}) custom-call(s32[48]{0:T(128)S(1)} %reshape.3.wanted_ref, bf16[3,8,2048]{2,1,0:T(8,128)(2,1)S(1)} %copy-done.2), custom_call_target="tpu_custom_call" | custom-call | tf_op jit(solution)/shard_map/fetch_tiles/pallas_call | solution.py:284
  18.2 0.0 copy-start.1
  18.2 0.7 copy-done.1
  18.9 41.7 %field_grad.1.sums_ref = bf16[16,3,16,128]{3,2,1,0:T(8,128)(2,1)} custom-call(s32[3,512]{1,0:T(4,128)} %slots_ref.1, bf16[16,3,16,128]{3,2,1,0:T(8,128)(2,1)} %copy-done.1, f32[32,64]{1,0:T(8,128)} %win_ref.1, f32[4,64]{1,0:T(4,128)} %bitcast.1, f32[1,4,256]{2,1,0:T(4,128)} %grad_ref.1, s32[3,65536]{1,0:T(4,128)} %corner_ref.1, f32[3,2,65536]{2,1,0:T(2,128)} %fraction_ref.1, ...), custom_call_target="tpu_custom_call" | custom-call | tf_op jit(solution)/shard_map/field_grad/pallas_call | solution.py:171
  60.6 0.0 copy-start
  60.6 0.9 %copy-done = bf16[16,3,16,128]{3,2,1,0:T(8,128)(2,1)S(1)} copy-done((bf16[16,3,16,128]{3,2,1,0:T(8,128)(2,1)S(1)}, bf16[16,3,16,128]{3,2,1,0:T(8,128)(2,1)}, u32[]{:S(2)}) %copy-start) | copy-done | bytes 196632
  61.5 7.4 %give_back.1 = f32[3,8,2048]{2,1,0:T(8,128)S(1)} custom-call(bf16[16,3,16,128]{3,2,1,0:T(8,128)(2,1)S(1)} %copy-done, f32[16,8,128]{2,1,0:T(8,128)S(1)} %get-tuple-element.8.asked_ref), custom_call_target="tpu_custom_call" | custom-call | tf_op jit(solution)/shard_map/give_back/pallas_call | solution.py:364
  68.9 0.7 copy.11
Async XLA Ops:
  0.8 0.9 %copy-start.2 = (bf16[3,8,2048]{2,1,0:T(8,128)(2,1)S(1)}, bf16[3,8,2048]{2,1,0:T(8,128)(2,1)}, u32[]{:S(2)}) copy-start(bf16[3,8,2048]{2,1,0:T(8,128)(2,1)} %planes_ref.1) | copy-start | bytes 294916
  18.2 0.7 copy-start.1
  60.6 0.9 %copy-start = (bf16[16,3,16,128]{3,2,1,0:T(8,128)(2,1)S(1)}, bf16[16,3,16,128]{3,2,1,0:T(8,128)(2,1)}, u32[]{:S(2)}) copy-start(bf16[16,3,16,128]{3,2,1,0:T(8,128)(2,1)} %field_grad.1.sums_ref) | copy-start | bytes 589828
